TPU v7x, 128 devices: a whole 4x4x4 slice. The times are simulated.
128 devices in a mesh: dp: 4 (over x_hi, core), tensor: 32 (over z, y, x_lo).
Axes of the slice: x: 4 (x_hi: 2, x_lo: 2; x = x_hi * 2 + x_lo), y: 4, z: 4, core: 2. Of those that a mesh axis runs over, the one named last changes fastest.
Arguments:
- grad_act: bfloat16 [8192, 8192], P(('dp', 'tensor')), parts along dimension 0, may hold values from -6 to 6
- x_pre: bfloat16 [8192, 8192], P(('dp', 'tensor')), parts along dimension 0, may hold values from -6 to 6
- grad_gate: bfloat16 [8192, 8192], P('dp', 'tensor'), parts along dimension 0, may hold values from -6 to 6
- normed_input: bfloat16 [8192, 4096], P('dp'), parts along dimension 0, may hold values from -0.125 to 0.125
- conv_weight: float32 [4, 8192], P(None, 'tensor'), may hold values from -3 to 3
- conv_bias: float32 [8192], P('tensor'), may hold values from -1 to 1
- up_x: bfloat16 [4096, 8192], P(None, 'tensor'), may hold values from -0.09375 to 0.09375
- up_z: bfloat16 [4096, 8192], P(None, 'tensor'), may hold values from -0.09375 to 0.09375
Outputs:
- grad_input: bfloat16 [8192, 4096], P(('dp', 'tensor')), parts along dimension 0
- grad_up_x: float32 [16384, 8192], P('dp', 'tensor'), parts along dimension 0
- grad_up_z: float32 [16384, 8192], P('dp', 'tensor'), parts along dimension 0
- grad_conv_weight: float32 [16, 8192], P('dp', 'tensor'), parts along dimension 0
- grad_conv_bias: float32 [32768], P(('dp', 'tensor')), parts along dimension 0
There are 4 independent parts, one for each index of `dp`. A program takes and returns all parts, laid end to end along the dimension named above; an argument that names none is the same for every part. Nothing has to cross between parts.
All inputs are finite; a program needn't handle non-finite values.
Results may differ from a plain program's by a relative error of at most 0.0065.
Values may be sent and summed in bfloat16 or wider, within the bound.
A program may use at most 192 MiB of HBM per device.

v0:
```python
import jax
import jax.numpy as jnp
from jax import lax
from jax.sharding import PartitionSpec as P

KERNEL = 4


def cell_gradient(inputs_pad, incoming, weights, bias_row, row_count):
    conv_value = bias_row[None, :] + sum(
        (
            weights[offset][None, :]
            * inputs_pad[KERNEL - 1 - offset : KERNEL - 1 - offset + row_count]
            for offset in range(KERNEL)
        )
    )
    gate_sig = jax.nn.sigmoid(conv_value)
    return (incoming.astype(jnp.float32) * gate_sig * (1.0 + conv_value * (1.0 - gate_sig))).astype(
        jnp.bfloat16
    )


def input_gradient(cell_pad, weights, row_count):
    return sum(
        (
            weights[offset][None, :] * cell_pad[offset : offset + row_count]
            for offset in range(KERNEL)
        )
    ).astype(jnp.bfloat16)


def tap_sums(inputs_pad, cell_float, row_count):
    return jnp.stack(
        [
            jnp.sum(
                inputs_pad[KERNEL - 1 - offset : KERNEL - 1 - offset + row_count] * cell_float,
                axis=0,
            )
            for offset in range(KERNEL)
        ]
    )


def per_device(grad_act, x_pre, grad_gate, normed_input, conv_weight, conv_bias, up_x, up_z):
    incoming, saved = (
        lax.all_to_all(grad_act, "tensor", split_axis=1, concat_axis=0, tiled=True),
        lax.all_to_all(x_pre, "tensor", split_axis=1, concat_axis=0, tiled=True),
    )
    row_count = incoming.shape[0]
    width = incoming.shape[1]
    inputs_pad = jnp.concatenate(
        [jnp.zeros((KERNEL - 1, width), jnp.float32), saved.astype(jnp.float32)], axis=0
    )
    cell_grad = cell_gradient(inputs_pad, incoming, conv_weight, conv_bias, row_count)
    cell_float = cell_grad.astype(jnp.float32)
    cell_pad = jnp.concatenate([cell_float, jnp.zeros((KERNEL - 1, width), jnp.float32)], axis=0)
    grad_x = input_gradient(cell_pad, conv_weight, row_count)
    weight_grad = tap_sums(inputs_pad, cell_float, row_count)
    bias_grad = jnp.sum(cell_float, axis=0)
    over_tokens = (((0,), (0,)), ((), ()))
    grad_up_x = lax.dot_general(
        normed_input, grad_x, over_tokens, preferred_element_type=jnp.float32
    )
    grad_up_z = lax.dot_general(
        normed_input, grad_gate, over_tokens, preferred_element_type=jnp.float32
    )
    contract = (((1,), (1,)), ((), ()))
    term = lax.dot_general(grad_x, up_x, contract, preferred_element_type=jnp.float32)
    result_rows = lax.psum_scatter(
        term + lax.dot_general(grad_gate, up_z, contract, preferred_element_type=jnp.float32),
        "tensor",
        scatter_dimension=0,
        tiled=True,
    ).astype(jnp.bfloat16)
    return (result_rows, grad_up_x, grad_up_z, weight_grad, bias_grad)


def solution(mesh):
    placed = (
        P(("dp", "tensor"), None),
        P(("dp", "tensor"), None),
        P("dp", "tensor"),
        P("dp", None),
        P(None, "tensor"),
        P("tensor"),
        P(None, "tensor"),
        P(None, "tensor"),
    )
    return jax.shard_map(
        per_device,
        mesh=mesh,
        in_specs=placed,
        out_specs=(
            P(("dp", "tensor"), None),
            P("dp", "tensor"),
            P("dp", "tensor"),
            P("dp", "tensor"),
            P(("dp", "tensor")),
        ),
        check_vma=False,
    )
```

profile of v0, /device:TPU:0, one launch (start us, length us, event | category | flops | bytes accessed | tf_op | source)
XLA Modules:
  0.0 822.7 jit_solution(1862971008638720651)
XLA Ops:
  7.2 0.0 copy-start
  7.2 2.5 copy.25
  9.7 9.3 %all-to-all-start.1 = ((bf16[64,32,256]{2,0,1:T(8,128)(2,1)}), bf16[64,32,256]{2,0,1:T(8,128)(2,1)S(1)}, u32[]{:S(2)}, u32[]{:S(2)}) async-start(bf16[64,32,256]{2,0,1:T(8,128)(2,1)} %bitcast.41), calls=%async_computation.1 | async-start | bytes 2097152 | tf_op jit(solution)/shard_map/all_to_all | solution.py:47
  19.0 0.0 copy-start.4
  19.0 2.3 copy.26
  21.3 15.5 %all-to-all-done.1 = bf16[64,32,256]{2,0,1:T(8,128)(2,1)S(1)} async-done(((bf16[64,32,256]{2,0,1:T(8,128)(2,1)}), bf16[64,32,256]{2,0,1:T(8,128)(2,1)S(1)}, u32[]{:S(2)}, u32[]{:S(2)}) %all-to-all-start.1) | async-done | bytes 1048608 | tf_op jit(solution)/shard_map/all_to_all | solution.py:47
  36.9 4.7 all-to-all-start
  41.6 0.0 copy-start.5
  41.6 0.0 reduce-scatter.2.cloned.1.call-start
  41.6 0.0 copy-done.4
  41.6 1.6 convert_element_type.43
  43.2 15.0 %all-to-all-done = bf16[64,32,256]{2,0,1:T(8,128)(2,1)} async-done(((bf16[64,32,256]{2,0,1:T(8,128)(2,1)}), bf16[64,32,256]{2,0,1:T(8,128)(2,1)}, u32[]{:S(2)}, u32[]{:S(2)}) %all-to-all-start) | async-done | bytes 1048608 | tf_op jit(solution)/shard_map/all_to_all | solution.py:46
  58.3 0.0 copy-done.5
  58.3 8.5 %convert_reduce_fusion = (f32[256]{0:T(256)}, f32[256]{0:T(256)S(1)}, f32[256]{0:T(256)S(1)}, f32[256]{0:T(256)S(1)}, f32[256]{0:T(256)S(1)}, /*index=5*/bf16[2048,256]{1,0:T(8,128)(2,1)S(1)}) fusion(bf16[64,32,256]{2,0,1:T(8,128)(2,1)S(1)} %all-to-all-done.1, f32[2048,256]{1,0:T(8,128)} %bitcast.39, f32[256]{0:T(256)S(1)} %bitcast.48, f32[256]{0:T(256)S(1)} %bitcast.50, ...), kind=kLoop, calls=%fused_computation.2 | loop fusion | flops 15203072 | bytes 5253120 | tf_op jit(solution)/shard_map/reduce_sum | solution.py:59
  66.7 0.2 convert_element_type.37
  66.9 1.0 fusion.3
  67.9 0.0 copy-done
  67.9 0.0 copy-start.2
  67.9 13.1 %fusion.12 = f32[2048,4096]{1,0:T(8,128)} fusion(bf16[2048,256]{1,0:T(8,128)(2,1)S(1)} %fusion.3, bf16[4096,256]{1,0:T(8,128)(2,1)S(1)} %copy-done), kind=kOutput, calls=%fused_computation.25 | convolution fusion | flops 4294967296 | bytes 36700160 | tf_op jit(solution)/shard_map/dot_general | solution.py:68
  81.0 0.0 copy-done.2
  81.0 25.0 %convolution_add_fusion = f32[2048,4096]{1,0:T(8,128)} fusion(f32[2048,4096]{1,0:T(8,128)} %fusion.12, bf16[2048,256]{1,0:T(8,128)(2,1)S(1)} %copy-done.2, bf16[4096,256]{1,0:T(8,128)(2,1)} %param.15), kind=kOutput, calls=%fused_computation | convolution fusion | flops 4303355904 | bytes 70254592 | tf_op jit(solution)/shard_map/dot_general | solution.py:70
  106.1 0.0 copy-start.3
  106.1 0.0 reduce-scatter.2.cloned.1.call-update
  106.1 1.2 copy-done.3
  107.3 11.0 %fusion.13 = f32[4096,256]{1,0:T(8,128)} fusion(bf16[2048,4096]{1,0:T(8,128)(2,1)} %param.11, bf16[2048,256]{1,0:T(8,128)(2,1)S(1)} %copy-done.3), kind=kOutput, calls=%fused_computation.26 | convolution fusion | flops 4294967296 | bytes 22020096 | tf_op jit(solution)/shard_map/dot_general | solution.py:64
  118.3 10.3 %convolution_bitcast_fusion = f32[4096,256]{0,1:T(8,128)} fusion(bf16[2048,256]{1,0:T(8,128)(2,1)S(1)} %fusion.3, bf16[2048,4096]{1,0:T(8,128)(2,1)} %param.11), kind=kOutput, calls=%fused_computation.1 | convolution fusion | flops 4294967296 | bytes 22020096 | tf_op jit(solution)/shard_map/dot_general | solution.py:61
  128.6 0.0 copy-start.1
  128.6 5.7 copy.20
  134.3 0.6 pad_maximum_fusion
  134.9 678.9 %reduce-scatter.2.cloned.1.call-done = f32[64,4096]{1,0:T(8,128)} async-done(((f32[2048,4096]{1,0:T(8,128)}), f32[64,4096]{1,0:T(8,128)}) %reduce-scatter.2.cloned.1.call-update) | async-done | bytes 1048592 | tf_op jit(solution)/shard_map/reduce_scatter | solution.py:69
  813.8 2.1 convert_element_type.39
  815.9 0.0 copy-done.1
  (1 shorter events, 0.0 us)
Async XLA Ops:
  7.2 60.7 %copy-start = (bf16[4096,256]{1,0:T(8,128)(2,1)S(1)}, bf16[4096,256]{1,0:T(8,128)(2,1)}, u32[]{:S(2)}) copy-start(bf16[4096,256]{1,0:T(8,128)(2,1)} %param.14) | copy-start | bytes 6291460
  9.7 27.2 %all-to-all-start.1 = ((bf16[64,32,256]{2,0,1:T(8,128)(2,1)}), bf16[64,32,256]{2,0,1:T(8,128)(2,1)S(1)}, u32[]{:S(2)}, u32[]{:S(2)}) async-start(bf16[64,32,256]{2,0,1:T(8,128)(2,1)} %bitcast.41), calls=%async_computation.1 | async-start | bytes 2097152 | tf_op jit(solution)/shard_map/all_to_all | solution.py:47
  19.0 22.6 %copy-start.4 = (f32[4,256]{1,0:T(4,128)S(1)}, f32[4,256]{1,0:T(4,128)}, u32[]{:S(2)}) copy-start(f32[4,256]{1,0:T(4,128)} %param.12) | copy-start | bytes 12292
  36.9 21.4 %all-to-all-start = ((bf16[64,32,256]{2,0,1:T(8,128)(2,1)}), bf16[64,32,256]{2,0,1:T(8,128)(2,1)}, u32[]{:S(2)}, u32[]{:S(2)}) async-start(bf16[64,32,256]{2,0,1:T(8,128)(2,1)} %bitcast.40), calls=%async_computation | async-start | bytes 2097152 | tf_op jit(solution)/shard_map/all_to_all | solution.py:46
  41.6 16.7 %copy-start.5 = (f32[256]{0:T(256)S(1)}, f32[256]{0:T(256)}, u32[]{:S(2)}) copy-start(f32[256]{0:T(256)} %param.13) | copy-start | bytes 3076
  41.6 772.2 %reduce-scatter.2.cloned.1.call-start = ((), (), s32[]{:S(2)}) async-start(), calls=%async_computation.3 | async-start | bytes 34603008 | tf_op jit(solution)/shard_map/reduce_scatter | solution.py:69
  67.9 13.1 %copy-start.2 = (bf16[2048,256]{1,0:T(8,128)(2,1)S(1)}, bf16[2048,256]{1,0:T(8,128)(2,1)}, u32[]{:S(2)}) copy-start(bf16[2048,256]{1,0:T(8,128)(2,1)} %param.10) | copy-start | bytes 3145732
  106.1 1.2 copy-start.3
  128.6 687.3 %copy-start.1 = (bf16[4096,256]{1,0:T(8,128)(2,1)S(1)}, bf16[4096,256]{1,0:T(8,128)(2,1)}, u32[]{:S(2)}) copy-start(bf16[4096,256]{1,0:T(8,128)(2,1)} %param.14) | copy-start | bytes 6291460
Sparse Core Ops, SparseCore 0:
  106.2 707.5 reduce-scatter.1
where the time goes:
time: 824 us; the launch traced here: 823 us
  waiting for transfers between devices  709 us (86%)
  matrix products  59.4 us (7%)
  starting transfers between devices  14.1 us (2%)
  between operations  14.1 us (2%)
  other arithmetic  13.9 us (2%)
  local copies, waits for them, and re-layouts  11.8 us (1%)
    reduce_scatter x1, waiting for transfers between devices, per_device(): lax.psum_scatter(term + lax.dot_general(grad_gate, up_z, contract, prefer...  679 us
    dot_general x1, matrix products, per_device(): lax.dot_general(grad_gate, up_z, contract, preferred_element_type=jnp.flo...  25 us
  transfers between devices with their start and end apart: 3, of which 3 were waited for; matrix products, arithmetic and copies ran while one was open for 4% of the time, Pallas kernels for 0%

commit v1 on v0

v1 whole, which is shorter than its diff:
```python
import jax
import jax.numpy as jnp
from jax import lax
from jax.experimental import pallas as pl
from jax.experimental.pallas import tpu as pltpu
from jax.sharding import PartitionSpec as P

MESH = pl.DeviceIdType.MESH
F32 = jnp.float32
BF16 = jnp.bfloat16
TAPS = 4
GROUP = 32
ROWS = 64
WIDTH = 256
DIM = 4096
TOKENS = GROUP * ROWS
CHUNKS = 4
CHUNK = DIM // CHUNKS
TILE = CHUNK // 4


def kernel(
    act_hbm,
    pre_hbm,
    gate_hbm,
    normed_hbm,
    taps_ref,
    bias_ref,
    upx_hbm,
    upz_hbm,
    out_ref,
    gux_hbm,
    guz_hbm,
    small_ref,
    act_buf,
    pre_buf,
    gate_buf,
    gate_t,
    gx_buf,
    gx_t,
    left,
    right,
    normed,
    stage,
    send1,
    recv1,
    send2,
    recv2,
    total,
    load_sem,
    a2a_send,
    a2a_recv,
    w_send,
    w_recv,
    fwd_send,
    fwd_recv,
    pair_send,
    pair_recv,
    stage_sem,
    s1_send,
    s1_recv,
    s2_send,
    s2_recv,
):
    dp = lax.axis_index("dp")
    me = lax.axis_index("tensor")
    z, y, x = me // 8, (me // 2) % 4, me % 2
    core = dp % 2
    partner = (dp, me + 1 - 2 * x)
    outside = ((dp + 2) % 4, me + 1 - 2 * x)
    sibling = (dp + 1 - 2 * core, me)

    def group_peer(step):
        return (me + step) % GROUP

    def local(src, dst, sem):
        return pltpu.make_async_copy(src, dst, sem)

    loads = [
        local(gate_hbm, gate_buf, load_sem.at[0]),
        local(normed_hbm, normed, load_sem.at[1]),
        local(gate_hbm.at[:, x], left.at[:, :, pl.ds(2 * WIDTH, WIDTH)], load_sem.at[2]),
        local(upx_hbm, right.at[:, pl.ds(0, WIDTH)], load_sem.at[3]),
        local(upz_hbm, right.at[:, pl.ds(2 * WIDTH, WIDTH)], load_sem.at[4]),
        local(
            act_hbm.at[:, pl.ds(pl.multiple_of(me * WIDTH, WIDTH), WIDTH)],
            act_buf.at[pl.ds(pl.multiple_of(me * ROWS, ROWS), ROWS)],
            load_sem.at[5],
        ),
        local(
            pre_hbm.at[:, pl.ds(pl.multiple_of(me * WIDTH, WIDTH), WIDTH)],
            pre_buf.at[pl.ds(pl.multiple_of(me * ROWS + 16, 16), ROWS)],
            load_sem.at[6],
        ),
    ]
    for copy in loads:
        copy.start()

    barrier = pltpu.get_barrier_semaphore()

    def greet(step, _):
        pl.semaphore_signal(
            barrier, inc=1, device_id=(dp, group_peer(step)), device_id_type=MESH
        )
        return 0

    lax.fori_loop(1, GROUP, greet, 0)
    pl.semaphore_signal(barrier, inc=1, device_id=outside, device_id_type=MESH)
    pl.semaphore_signal(barrier, inc=1, device_id=sibling, device_id_type=MESH)
    pl.semaphore_wait(barrier, GROUP + 1)

    def remote(src, dst, send, recv, device):
        return pltpu.make_async_remote_copy(
            src_ref=src,
            dst_ref=dst,
            send_sem=send,
            recv_sem=recv,
            device_id=device,
            device_id_type=MESH,
        )

    def weight_rows(q, half):
        return pl.ds(pl.multiple_of(q * CHUNK + half * (CHUNK // 2), CHUNK // 2), CHUNK // 2)

    def weight_copies(q):
        rows = weight_rows(q, core)
        return [
            remote(
                src.at[rows],
                right.at[rows, pl.ds(slot * WIDTH, WIDTH)],
                w_send.at[q, k],
                w_recv.at[q, k],
                outside,
            )
            for k, (src, slot) in enumerate(((upx_hbm, 1), (upz_hbm, 3)))
        ]

    def forward_copies(q):
        rows = weight_rows(q, core)
        return [
            remote(
                right.at[rows, pl.ds(slot * WIDTH, WIDTH)],
                right.at[rows, pl.ds(slot * WIDTH, WIDTH)],
                fwd_send.at[q, k],
                fwd_recv.at[q, k],
                sibling,
            )
            for k, slot in enumerate((1, 3))
        ]

    for copy in weight_copies(0):
        copy.start()

    def exchange(step, _):
        peer = group_peer(step)
        columns = pl.ds(pl.multiple_of(peer * WIDTH, WIDTH), WIDTH)
        remote(
            pre_hbm.at[:, columns],
            pre_buf.at[pl.ds(pl.multiple_of(me * ROWS + 16, 16), ROWS)],
            a2a_send.at[0],
            a2a_recv.at[0],
            (dp, peer),
        ).start()
        remote(
            act_hbm.at[:, columns],
            act_buf.at[pl.ds(pl.multiple_of(me * ROWS, ROWS), ROWS)],
            a2a_send.at[1],
            a2a_recv.at[1],
            (dp, peer),
        ).start()
        return 0

    lax.fori_loop(1, GROUP, exchange, 0)
    gate_pair = remote(
        gate_hbm.at[:, 1 - x],
        left.at[:, :, pl.ds(3 * WIDTH, WIDTH)],
        pair_send.at[0],
        pair_recv.at[0],
        partner,
    )
    gate_pair.start()
    for q in range(1, CHUNKS):
        for copy in weight_copies(q):
            copy.start()

    pre_buf[pl.ds(0, 16), :] = jnp.zeros((16, WIDTH), BF16)
    pre_buf[pl.ds(TOKENS + 16, 16), :] = jnp.zeros((16, WIDTH), BF16)
    act_buf[pl.ds(TOKENS, 16), :] = jnp.zeros((16, WIDTH), BF16)

    def up_gradient(n, slot, turned, result):
        columns = pl.ds(pl.multiple_of(n * 512, 512), 512)
        product = jnp.dot(turned[...], normed[:, columns], preferred_element_type=F32)
        stage[slot] = product.T
        local(stage.at[slot], result.at[columns], stage_sem.at[slot]).start()

    def stage_wait(slot):
        local(stage.at[slot], guz_hbm.at[pl.ds(0, 512)], stage_sem.at[slot]).wait()

    loads[0].wait()

    def turn_gate(b, _):
        pair = jnp.concatenate([gate_buf[b, 0], gate_buf[b, 1]], axis=0).astype(F32)
        gate_t[:, pl.ds(pl.multiple_of(b * 128, 128), 128)] = pair.T.astype(BF16)
        return 0

    lax.fori_loop(0, 16, turn_gate, 0)
    loads[1].wait()

    def gate_step(n, _):
        for slot in range(2):

            @pl.when(n > 0)
            def _():
                stage_wait(slot)

            up_gradient(2 * n + slot, slot, gate_t, guz_hbm)
        return 0

    lax.fori_loop(0, 4, gate_step, 0)

    def forward(q):
        for copy in weight_copies(q):
            copy.wait_recv()
        for copy in forward_copies(q):
            copy.start()

    forward(0)

    loads[5].wait()
    loads[6].wait()
    others = pl.ds(0, TOKENS - ROWS)
    local(pre_buf.at[others], pre_buf.at[others], a2a_recv.at[0]).wait()
    local(act_buf.at[others], act_buf.at[others], a2a_recv.at[1]).wait()

    def convolve(b, sums):
        sums = list(sums)
        for part in range(2):
            lanes = pl.ds(part * 128, 128)
            weights = [taps_ref[pl.ds(j, 1), lanes] for j in range(TAPS)]
            bias = bias_ref[:, lanes]
            halves = []
            for parity in range(2):
                row = pl.multiple_of(b * 128 + parity * ROWS, ROWS)
                window = pre_buf[pl.ds(row, 96), lanes].astype(F32)[8:88]
                incoming = act_buf[pl.ds(row, 80), lanes].astype(F32)[:72]
                shifted = [window[8:]] + [pltpu.roll(window, j, 0)[8:] for j in range(1, TAPS)]
                conv = bias + (
                    weights[0] * shifted[0]
                    + weights[1] * shifted[1]
                    + weights[2] * shifted[2]
                    + weights[3] * shifted[3]
                )
                sig = 1.0 / (1.0 + jnp.exp(-conv))
                cell = (incoming * sig * (1.0 + conv * (1.0 - sig))).astype(BF16).astype(F32)
                grad = weights[0] * cell[:ROWS]
                for j in range(1, TAPS):
                    grad += weights[j] * pltpu.roll(cell, 72 - j, 0)[:ROWS]
                grad = grad.astype(BF16)
                gx_buf[parity, b, :, lanes] = grad
                halves.append(grad.astype(F32))
                inner = cell[:ROWS]
                for j in range(TAPS):
                    k = part * 5 + j
                    sums[k] += (shifted[j][:ROWS] * inner).reshape(8, 8, 128).sum(0)
                sums[part * 5 + 4] += inner.reshape(8, 8, 128).sum(0)
            left[b, :, lanes] = jnp.where(x == 0, halves[0], halves[1]).astype(BF16)
        remote(
            gx_buf.at[1 - x, b],
            left.at[b, :, pl.ds(WIDTH, WIDTH)],
            pair_send.at[1],
            pair_recv.at[1],
            partner,
        ).start()
        return tuple(sums)

    zero = jnp.zeros((8, 128), F32)
    sums = lax.fori_loop(0, 16, convolve, (zero,) * 10)
    for part in range(2):
        rows = [sums[part * 5 + j].sum(0, keepdims=True) for j in range(5)]
        rows.append(jnp.zeros((3, 128), F32))
        small_ref[:, pl.ds(part * 128, 128)] = jnp.concatenate(rows, axis=0)

    def turn_gx(b, _):
        pair = jnp.concatenate([gx_buf[0, b], gx_buf[1, b]], axis=0).astype(F32)
        gx_t[:, pl.ds(pl.multiple_of(b * 128, 128), 128)] = pair.T.astype(BF16)
        return 0

    lax.fori_loop(0, 16, turn_gx, 0)

    def place(s, first):
        along_z = (1 - s) if first else s
        return along_z * z + (1 - along_z) * y

    def neighbour(s, first, step):
        along_z = (1 - s) if first else s
        far_z = (z + step * along_z) % 4
        far_y = (y + step * (1 - along_z)) % 4
        return (dp, (far_z * 4 + far_y) * 2 + x)

    def term(q, s, step, half):
        target = (place(s, True) + step) % 4
        base = target * (4 - 3 * s)
        stride = 1 + 3 * s
        rows = jnp.concatenate([left[base + stride * j] for j in range(4)], axis=0)
        columns = pl.ds(
            pl.multiple_of(q * CHUNK + s * (CHUNK // 2) + half * TILE, TILE), TILE
        )
        return lax.dot_general(
            rows, right[columns, :], (((1,), (1,)), ((), ())), preferred_element_type=F32
        )

    def hop1(q, s, k):
        step = 1 + 2 * (k % 2)
        return remote(
            send1.at[q, s, k],
            recv1.at[q, s, k],
            s1_send,
            s1_recv.at[q, s, k],
            neighbour(s, True, step),
        )

    def hop2(q, s, k):
        step = 1 + 2 * (k % 2)
        return remote(
            send2.at[q, s, k],
            recv2.at[q, s, k],
            s2_send,
            s2_recv.at[q, s, k],
            neighbour(s, False, step),
        )

    def first_terms(q):
        if q > 0:
            forward(q)
        for copy in forward_copies(q):
            copy.wait_recv()

        def body(i, _):
            k, s = i // 2, i % 2
            near = k // 2
            step = 2 - near + 2 * near * (k % 2)
            half = (k + near) % 2
            send1[q, s, k] = term(q, s, step, half).astype(BF16)
            hop1(q, s, k).start()
            return 0

        lax.fori_loop(0, 8, body, 0)

    def passed_terms(q):
        def body(i, _):
            half, s = i // 2, i % 2
            value = term(q, s, 1 + 2 * half, half)
            hop1(q, s, half).wait_recv()
            send1[q, s, 4 + half] = (value + recv1[q, s, half].astype(F32)).astype(BF16)
            hop1(q, s, 4 + half).start()
            return 0

        lax.fori_loop(0, 4, body, 0)

    def own_terms(q):
        def body(i, _):
            half, s = i // 2, i % 2
            value = term(q, s, 0, half)
            hop1(q, s, 4 - 2 * half).wait_recv()
            hop1(q, s, 3 + 2 * half).wait_recv()
            value += recv1[q, s, 4 - 2 * half].astype(F32)
            value += recv1[q, s, 3 + 2 * half].astype(F32)
            total[q, s, half] = value.reshape(4, ROWS, TILE)
            return 0

        lax.fori_loop(0, 4, body, 0)

        def spread(i, _):
            k, s = i // 2, i % 2
            near = k // 2
            step = 2 - near + 2 * near * (k % 2)
            half = (k + near) % 2
            send2[q, s, k] = total[q, s, half, (place(s, False) + step) % 4].astype(BF16)
            hop2(q, s, k).start()
            return 0

        lax.fori_loop(0, 8, spread, 0)

    def passed_rows(q):
        def body(i, _):
            half, s = i // 2, i % 2
            value = total[q, s, half, (place(s, False) + 1 + 2 * half) % 4]
            hop2(q, s, half).wait_recv()
            send2[q, s, 4 + half] = (value + recv2[q, s, half].astype(F32)).astype(BF16)
            hop2(q, s, 4 + half).start()
            return 0

        lax.fori_loop(0, 4, body, 0)

    def finish(q):
        for s in range(2):
            for half in range(2):
                value = total[q, s, half, place(s, False)]
                hop2(q, s, 4 - 2 * half).wait_recv()
                hop2(q, s, 3 + 2 * half).wait_recv()
                value += recv2[q, s, 4 - 2 * half].astype(F32)
                value += recv2[q, s, 3 + 2 * half].astype(F32)
                out_ref[:, pl.ds(q * CHUNK + s * (CHUNK // 2) + half * TILE, TILE)] = (
                    value.astype(BF16)
                )

    def gx_step(n):
        for slot in range(2):
            stage_wait(slot)
            up_gradient(2 * n + slot, slot, gx_t, gux_hbm)

    for i in (2, 3, 4):
        loads[i].wait()
    gate_pair.wait_recv()
    own_part = left.at[:, :, pl.ds(WIDTH, WIDTH)]
    local(own_part, own_part, pair_recv.at[1]).wait()

    first_terms(0)
    first_terms(1)
    passed_terms(0)
    first_terms(2)
    passed_terms(1)
    gx_step(0)
    own_terms(0)
    first_terms(3)
    passed_terms(2)
    gx_step(1)
    own_terms(1)
    passed_rows(0)
    passed_terms(3)
    gx_step(2)
    own_terms(2)
    passed_rows(1)
    finish(0)
    gx_step(3)
    own_terms(3)
    passed_rows(2)
    finish(1)
    passed_rows(3)
    finish(2)
    finish(3)

    for k in range(2):
        local(pre_buf.at[others], pre_buf.at[others], a2a_send.at[k]).wait()
    gate_pair.wait_send()
    local(gx_buf.at[0], gx_buf.at[0], pair_send.at[1]).wait()
    for q in range(CHUNKS):
        for copy in weight_copies(q) + forward_copies(q):
            copy.wait_send()
    local(send1, send1, s1_send).wait()
    local(send2, send2, s2_send).wait()
    for slot in range(2):
        stage_wait(slot)


def per_device(grad_act, x_pre, grad_gate, normed_input, conv_weight, conv_bias, up_x, up_z):
    anywhere = pl.BlockSpec(memory_space=pl.ANY)
    vmem = pl.BlockSpec(memory_space=pltpu.VMEM)
    dma = pltpu.SemaphoreType.DMA
    out, gux, guz, small = pl.pallas_call(
        kernel,
        out_shape=(
            jax.ShapeDtypeStruct((ROWS, DIM), BF16),
            jax.ShapeDtypeStruct((DIM, WIDTH), F32),
            jax.ShapeDtypeStruct((DIM, WIDTH), F32),
            jax.ShapeDtypeStruct((8, WIDTH), F32),
        ),
        in_specs=[anywhere] * 4 + [vmem] * 2 + [anywhere] * 2,
        out_specs=(vmem, anywhere, anywhere, vmem),
        scratch_shapes=[
            pltpu.VMEM((TOKENS + 16, WIDTH), BF16),
            pltpu.VMEM((TOKENS + 32, WIDTH), BF16),
            pltpu.VMEM((16, 2, ROWS, WIDTH), BF16),
            pltpu.VMEM((WIDTH, TOKENS), BF16),
            pltpu.VMEM((2, 16, ROWS, WIDTH), BF16),
            pltpu.VMEM((WIDTH, TOKENS), BF16),
            pltpu.VMEM((16, ROWS, 4 * WIDTH), BF16),
            pltpu.VMEM((DIM, 4 * WIDTH), BF16),
            pltpu.VMEM((TOKENS, DIM), BF16),
            pltpu.VMEM((2, 512, WIDTH), F32),
            pltpu.VMEM((CHUNKS, 2, 6, 256, TILE), BF16),
            pltpu.VMEM((CHUNKS, 2, 6, 256, TILE), BF16),
            pltpu.VMEM((CHUNKS, 2, 6, ROWS, TILE), BF16),
            pltpu.VMEM((CHUNKS, 2, 6, ROWS, TILE), BF16),
            pltpu.VMEM((CHUNKS, 2, 2, 4, ROWS, TILE), F32),
            dma((7,)),
            dma((2,)),
            dma((2,)),
            dma((CHUNKS, 2)),
            dma((CHUNKS, 2)),
            dma((CHUNKS, 2)),
            dma((CHUNKS, 2)),
            dma((2,)),
            dma((2,)),
            dma((2,)),
            dma,
            dma((CHUNKS, 2, 6)),
            dma,
            dma((CHUNKS, 2, 6)),
        ],
        compiler_params=pltpu.CompilerParams(
            collective_id=0, has_side_effects=True, vmem_limit_bytes=62 * 1024 * 1024
        ),
        name="conv_up_backward",
    )(
        grad_act,
        x_pre,
        grad_gate.reshape(16, 2, ROWS, WIDTH),
        normed_input,
        conv_weight,
        conv_bias.reshape(1, WIDTH),
        up_x,
        up_z,
    )
    return out, gux, guz, small[:TAPS], small[TAPS]


def solution(mesh):
    placed = (
        P(("dp", "tensor"), None),
        P(("dp", "tensor"), None),
        P("dp", "tensor"),
        P("dp", None),
        P(None, "tensor"),
        P("tensor"),
        P(None, "tensor"),
        P(None, "tensor"),
    )
    return jax.shard_map(
        per_device,
        mesh=mesh,
        in_specs=placed,
        out_specs=(
            P(("dp", "tensor"), None),
            P("dp", "tensor"),
            P("dp", "tensor"),
            P("dp", "tensor"),
            P(("dp", "tensor")),
        ),
        check_vma=False,
    )
```

time: 824 us -> 119 us (0.14)
  waiting for transfers between devices: 709 us -> 0 us
  Pallas kernels: 0 us -> 106 us
  matrix products: 59.4 us -> 0 us
  starting transfers between devices: 14.1 us -> 0 us
  other arithmetic: 13.9 us -> 0 us
  between operations: 14.1 us -> 0.65 us
    reduce_scatter x1 -> x0, waiting for transfers between devices: 679 us -> none  [per_device(): lax.psum_scatter(term + lax.dot_general(grad_gate, up_z, contract, prefer...]
    pallas_call x0 -> x1, Pallas kernels: none -> 106 us  [per_device(): pl.pallas_call(kernel, out_shape=(jax.ShapeDtypeStruct((ROWS, DIM), BF16)...]
    dot_general x4 -> x0, matrix products: 59.4 us -> none  [the longest x1 25 us: per_device(): lax.dot_general(grad_gate, up_z, contract, preferred_element_type=jnp.flo...]
    all_to_all x2 -> x0, waiting for transfers between devices: 30.6 us -> none  [the longest x1 15.5 us: per_device(): lax.all_to_all(x_pre, 'tensor', split_axis=1, concat_axis=0, tiled=True)]
    all_to_all x2 -> x0, starting transfers between devices: 14 us -> none  [the longest x1 9.35 us: per_device(): lax.all_to_all(x_pre, 'tensor', split_axis=1, concat_axis=0, tiled=True)]
    reduce_sum x1 -> x0, other arithmetic: 8.46 us -> none  [per_device(): bias_grad = jnp.sum(cell_float, axis=0)]
  transfers between devices with their start and end apart: 3 -> 0, of which waited for: 3 -> 0; matrix products, arithmetic and copies ran while one was open for 4% -> 0% of each run, Pallas kernels for 0% -> 0%
where the time goes in v1:
time: 119 us; the launch traced here: 117 us
  Pallas kernels  106 us (89%)
  local copies, waits for them, and re-layouts  11.1 us (9%)
    pallas_call x1, Pallas kernels, per_device(): pl.pallas_call(kernel, out_shape=(jax.ShapeDtypeStruct((ROWS, DIM), BF16)...  106 us
    unnamed x5, local copies, waits for them, and re-layouts  8.52 us
    slice x2, local copies, waits for them, and re-layouts, per_device(): return (out, gux, guz, small[:TAPS], small[TAPS])  2.55 us

profile of v1, /device:TPU:0, one launch (start us, length us, event | category | flops | bytes accessed | tf_op | source)
XLA Modules:
  0.0 117.4 jit_solution(16982362416546368395)
XLA Ops:
  0.6 105.7 %conv_up_backward.1 = (bf16[64,4096]{1,0:T(8,128)(2,1)}, f32[4096,256]{1,0:T(8,128)}, f32[4096,256]{1,0:T(8,128)}, f32[8,256]{1,0:T(8,128)}) custom-call(bf16[64,8192]{1,0:T(8,128)(2,1)} %act_hbm.1, bf16[64,8192]{1,0:T(8,128)(2,1)} %pre_hbm.1, bf16[16,2,64,256]{3,2,1,0:T(8,128)(2,1)} %bitcast.3, bf16[2048,4096]{1,0:T(8,128)(2,1)} %normed_hbm.1, ...), custom_call_target="tpu_custom_call" | custom-call | tf_op jit(solution)/shard_map/conv_up_backward/pallas_call | solution.py:460
  106.3 1.3 %slice.7 = f32[1,256]{1,0:T(1,128)} slice(f32[8,256]{1,0:T(8,128)} %get-tuple-element.12), slice={[4:5], [0:256]} | slice | bytes 2048 | tf_op jit(solution)/shard_map/slice | solution.py:515
  107.6 1.3 %slice.6 = f32[4,256]{1,0:T(4,128)} slice(f32[8,256]{1,0:T(8,128)} %get-tuple-element.12), slice={[0:4], [0:256]} | slice | bytes 8192 | tf_op jit(solution)/shard_map/slice | solution.py:515
  108.9 1.9 %copy.16 = bf16[64,4096]{1,0:T(8,128)(2,1)} copy(bf16[64,4096]{1,0:T(8,128)(2,1)} %get-tuple-element.18) | data formatting | bytes 1048576
  110.7 0.0 copy-start
  110.8 4.6 %copy.17 = f32[4096,256]{1,0:T(8,128)} copy(f32[4096,256]{1,0:T(8,128)} %get-tuple-element.19) | data formatting | bytes 8388608
  115.4 0.0 copy-done
  115.4 2.0 %copy.18 = f32[4096,256]{1,0:T(8,128)} copy(f32[4096,256]{1,0:T(8,128)S(1)} %copy-done) | data formatting | bytes 8388608
Async XLA Ops:
  110.7 4.6 %copy-start = (f32[4096,256]{1,0:T(8,128)S(1)}, f32[4096,256]{1,0:T(8,128)}, u32[]{:S(2)}) copy-start(f32[4096,256]{1,0:T(8,128)} %get-tuple-element.20) | copy-start | bytes 12582916

commit v2 on v1

--- a/solution.py
+++ b/solution.py
@@ -13,6 +13,8 @@
 ROWS = 64
 WIDTH = 256
 DIM = 4096
+INNER = 8192
+HALF = INNER // 2
 TOKENS = GROUP * ROWS
 CHUNKS = 4
 CHUNK = DIM // CHUNKS
@@ -34,9 +36,17 @@
     small_ref,
     act_buf,
     pre_buf,
-    gate_buf,
+    tail_out,
+    tail_in,
+    head_out,
+    head_in,
+    params,
+    sums_out,
+    sums_in,
+    gate_far,
     gate_t,
-    gx_buf,
+    gx_out,
+    gx_far,
     gx_t,
     left,
     right,
@@ -48,8 +58,14 @@
     recv2,
     total,
     load_sem,
-    a2a_send,
-    a2a_recv,
+    param_send,
+    param_recv,
+    halo_send,
+    halo_recv,
+    gx_send,
+    gx_recv,
+    sums_send,
+    sums_recv,
     w_send,
     w_recv,
     fwd_send,
@@ -65,6 +81,7 @@
     dp = lax.axis_index("dp")
     me = lax.axis_index("tensor")
     z, y, x = me // 8, (me // 2) % 4, me % 2
+    spot = me // 2
     core = dp % 2
     partner = (dp, me + 1 - 2 * x)
     outside = ((dp + 2) % 4, me + 1 - 2 * x)
@@ -75,39 +92,6 @@
 
     def local(src, dst, sem):
         return pltpu.make_async_copy(src, dst, sem)
-
-    loads = [
-        local(gate_hbm, gate_buf, load_sem.at[0]),
-        local(normed_hbm, normed, load_sem.at[1]),
-        local(gate_hbm.at[:, x], left.at[:, :, pl.ds(2 * WIDTH, WIDTH)], load_sem.at[2]),
-        local(upx_hbm, right.at[:, pl.ds(0, WIDTH)], load_sem.at[3]),
-        local(upz_hbm, right.at[:, pl.ds(2 * WIDTH, WIDTH)], load_sem.at[4]),
-        local(
-            act_hbm.at[:, pl.ds(pl.multiple_of(me * WIDTH, WIDTH), WIDTH)],
-            act_buf.at[pl.ds(pl.multiple_of(me * ROWS, ROWS), ROWS)],
-            load_sem.at[5],
-        ),
-        local(
-            pre_hbm.at[:, pl.ds(pl.multiple_of(me * WIDTH, WIDTH), WIDTH)],
-            pre_buf.at[pl.ds(pl.multiple_of(me * ROWS + 16, 16), ROWS)],
-            load_sem.at[6],
-        ),
-    ]
-    for copy in loads:
-        copy.start()
-
-    barrier = pltpu.get_barrier_semaphore()
-
-    def greet(step, _):
-        pl.semaphore_signal(
-            barrier, inc=1, device_id=(dp, group_peer(step)), device_id_type=MESH
-        )
-        return 0
-
-    lax.fori_loop(1, GROUP, greet, 0)
-    pl.semaphore_signal(barrier, inc=1, device_id=outside, device_id_type=MESH)
-    pl.semaphore_signal(barrier, inc=1, device_id=sibling, device_id_type=MESH)
-    pl.semaphore_wait(barrier, GROUP + 1)
 
     def remote(src, dst, send, recv, device):
         return pltpu.make_async_remote_copy(
@@ -118,6 +102,70 @@
             device_id=device,
             device_id_type=MESH,
         )
+
+    loads = [
+        local(pre_hbm, pre_buf, load_sem.at[0]),
+        local(act_hbm, act_buf, load_sem.at[1]),
+        local(gate_hbm.at[:, x], left.at[:, :, pl.ds(2 * WIDTH, WIDTH)], load_sem.at[2]),
+        local(gate_hbm.at[:, 1 - x], gate_far, load_sem.at[3]),
+        local(normed_hbm.at[:, x], normed.at[:, 0], load_sem.at[4]),
+        local(normed_hbm.at[:, 1 - x], normed.at[:, 1], load_sem.at[5]),
+        local(upx_hbm, right.at[:, pl.ds(0, WIDTH)], load_sem.at[6]),
+        local(upz_hbm, right.at[:, pl.ds(2 * WIDTH, WIDTH)], load_sem.at[7]),
+    ]
+    for copy in loads:
+        copy.start()
+
+    barrier = pltpu.get_barrier_semaphore()
+
+    def greet(step, _):
+        pl.semaphore_signal(
+            barrier, inc=1, device_id=(dp, group_peer(step)), device_id_type=MESH
+        )
+        return 0
+
+    lax.fori_loop(1, GROUP, greet, 0)
+    pl.semaphore_signal(barrier, inc=1, device_id=outside, device_id_type=MESH)
+    pl.semaphore_signal(barrier, inc=1, device_id=sibling, device_id_type=MESH)
+
+    loads[0].wait()
+    loads[1].wait()
+    top = lax.broadcasted_iota(jnp.int32, (8, 1024), 0) < 4
+    for part in range(4):
+        low = pl.ds(part * 1024, 1024)
+        high = pl.ds(HALF + part * 1024, 1024)
+        last = pre_buf[pl.ds(48, 16), low].astype(F32)[8:]
+        last_high = pre_buf[pl.ds(48, 16), high].astype(F32)[8:]
+        last = jnp.where(top, pltpu.roll(last, 4, 0), last_high)
+        tail_out[part // 2, :, pl.ds((part % 2) * 1024, 1024)] = last
+        first = []
+        for buf in (pre_buf, act_buf):
+            rows = buf[pl.ds(0, 16), low].astype(F32)[:8]
+            rows_high = buf[pl.ds(0, 16), high].astype(F32)[:8]
+            first.append(jnp.where(top, rows, pltpu.roll(rows_high, 4, 0)))
+        head_out[:, low] = jnp.concatenate(first, axis=0).astype(BF16)
+    params[me, pl.ds(0, TAPS), :] = taps_ref[...]
+    params[me, pl.ds(TAPS, 1), :] = bias_ref[...]
+    params[me, pl.ds(TAPS + 1, 3), :] = jnp.zeros((3, WIDTH), F32)
+
+    pl.semaphore_wait(barrier, GROUP + 1)
+
+    tail = remote(
+        tail_out, tail_in, halo_send.at[0], halo_recv.at[0], (dp, group_peer(1))
+    )
+    head = remote(
+        head_out, head_in, halo_send.at[1], halo_recv.at[1], (dp, group_peer(GROUP - 1))
+    )
+    tail.start()
+    head.start()
+
+    def share(step, _):
+        remote(
+            params.at[me], params.at[me], param_send, param_recv, (dp, group_peer(step))
+        ).start()
+        return 0
+
+    lax.fori_loop(1, GROUP, share, 0)
 
     def weight_rows(q, half):
         return pl.ds(pl.multiple_of(q * CHUNK + half * (CHUNK // 2), CHUNK // 2), CHUNK // 2)
@@ -148,101 +196,64 @@
             for k, slot in enumerate((1, 3))
         ]
 
-    for copy in weight_copies(0):
-        copy.start()
-
-    def exchange(step, _):
-        peer = group_peer(step)
-        columns = pl.ds(pl.multiple_of(peer * WIDTH, WIDTH), WIDTH)
-        remote(
-            pre_hbm.at[:, columns],
-            pre_buf.at[pl.ds(pl.multiple_of(me * ROWS + 16, 16), ROWS)],
-            a2a_send.at[0],
-            a2a_recv.at[0],
-            (dp, peer),
-        ).start()
-        remote(
-            act_hbm.at[:, columns],
-            act_buf.at[pl.ds(pl.multiple_of(me * ROWS, ROWS), ROWS)],
-            a2a_send.at[1],
-            a2a_recv.at[1],
-            (dp, peer),
-        ).start()
-        return 0
-
-    lax.fori_loop(1, GROUP, exchange, 0)
-    gate_pair = remote(
-        gate_hbm.at[:, 1 - x],
-        left.at[:, :, pl.ds(3 * WIDTH, WIDTH)],
-        pair_send.at[0],
-        pair_recv.at[0],
-        partner,
-    )
-    gate_pair.start()
-    for q in range(1, CHUNKS):
+    for q in range(CHUNKS):
         for copy in weight_copies(q):
             copy.start()
 
-    pre_buf[pl.ds(0, 16), :] = jnp.zeros((16, WIDTH), BF16)
-    pre_buf[pl.ds(TOKENS + 16, 16), :] = jnp.zeros((16, WIDTH), BF16)
-    act_buf[pl.ds(TOKENS, 16), :] = jnp.zeros((16, WIDTH), BF16)
-
     def up_gradient(n, slot, turned, result):
         columns = pl.ds(pl.multiple_of(n * 512, 512), 512)
-        product = jnp.dot(turned[...], normed[:, columns], preferred_element_type=F32)
+        rows = normed[:, :, :, columns].reshape(TOKENS, 512)
+        product = jnp.dot(turned[...], rows, preferred_element_type=F32)
         stage[slot] = product.T
         local(stage.at[slot], result.at[columns], stage_sem.at[slot]).start()
 
     def stage_wait(slot):
         local(stage.at[slot], guz_hbm.at[pl.ds(0, 512)], stage_sem.at[slot]).wait()
 
-    loads[0].wait()
+    loads[2].wait()
+    loads[3].wait()
 
     def turn_gate(b, _):
-        pair = jnp.concatenate([gate_buf[b, 0], gate_buf[b, 1]], axis=0).astype(F32)
+        near = left[b, :, pl.ds(2 * WIDTH, WIDTH)]
+        pair = jnp.concatenate([near, gate_far[b]], axis=0).astype(F32)
         gate_t[:, pl.ds(pl.multiple_of(b * 128, 128), 128)] = pair.T.astype(BF16)
         return 0
 
     lax.fori_loop(0, 16, turn_gate, 0)
-    loads[1].wait()
-
-    def gate_step(n, _):
-        for slot in range(2):
-
-            @pl.when(n > 0)
-            def _():
-                stage_wait(slot)
-
-            up_gradient(2 * n + slot, slot, gate_t, guz_hbm)
-        return 0
-
-    lax.fori_loop(0, 4, gate_step, 0)
-
-    def forward(q):
-        for copy in weight_copies(q):
-            copy.wait_recv()
-        for copy in forward_copies(q):
-            copy.start()
-
-    forward(0)
-
-    loads[5].wait()
-    loads[6].wait()
-    others = pl.ds(0, TOKENS - ROWS)
-    local(pre_buf.at[others], pre_buf.at[others], a2a_recv.at[0]).wait()
-    local(act_buf.at[others], act_buf.at[others], a2a_recv.at[1]).wait()
-
-    def convolve(b, sums):
-        sums = list(sums)
-        for part in range(2):
-            lanes = pl.ds(part * 128, 128)
-            weights = [taps_ref[pl.ds(j, 1), lanes] for j in range(TAPS)]
-            bias = bias_ref[:, lanes]
-            halves = []
-            for parity in range(2):
-                row = pl.multiple_of(b * 128 + parity * ROWS, ROWS)
-                window = pre_buf[pl.ds(row, 96), lanes].astype(F32)[8:88]
-                incoming = act_buf[pl.ds(row, 80), lanes].astype(F32)[:72]
+
+    tail.wait_recv()
+    head.wait_recv()
+    others = pl.ds(0, GROUP - 1)
+    local(params.at[others], params.at[others], param_recv).wait()
+
+    def convolve(i, _):
+        g = (spot + i) % 16
+        lower = g < 8
+        for block in range(2):
+            feature = 2 * g + (x + block) % 2
+            for part in range(2):
+                inner = pl.ds(part * 128, 128)
+                lane = pl.multiple_of(feature * WIDTH + part * 128, 128)
+                packed = pl.multiple_of((feature % 16) * WIDTH + part * 128, 128)
+                lanes = pl.ds(lane, 128)
+                weights = [params[feature, pl.ds(j, 1), inner] for j in range(TAPS)]
+                bias = params[feature, pl.ds(TAPS, 1), inner]
+                before = tail_in[
+                    (feature % 16) // 8,
+                    :,
+                    pl.ds(pl.multiple_of((feature % 8) * WIDTH + part * 128, 128), 128),
+                ]
+                before = jnp.where(lower, pltpu.roll(before, 4, 0), before)
+                before = jnp.where(me == 0, 0.0, before)
+                after = head_in[:, pl.ds(packed, 128)].astype(F32)
+                after_pre, after_act = after[:8], after[8:]
+                after_pre = jnp.where(lower, after_pre, pltpu.roll(after_pre, 4, 0))
+                after_act = jnp.where(lower, after_act, pltpu.roll(after_act, 4, 0))
+                after_act = jnp.where(me == GROUP - 1, 0.0, after_act)
+                window = jnp.concatenate(
+                    [before, pre_buf[:, lanes].astype(F32), after_pre], axis=0
+                )
+                incoming = jnp.concatenate([act_buf[:, lanes].astype(F32), after_act], axis=0)
                 shifted = [window[8:]] + [pltpu.roll(window, j, 0)[8:] for j in range(1, TAPS)]
                 conv = bias + (
                     weights[0] * shifted[0]
@@ -255,37 +266,67 @@
                 grad = weights[0] * cell[:ROWS]
                 for j in range(1, TAPS):
                     grad += weights[j] * pltpu.roll(cell, 72 - j, 0)[:ROWS]
-                grad = grad.astype(BF16)
-                gx_buf[parity, b, :, lanes] = grad
-                halves.append(grad.astype(F32))
-                inner = cell[:ROWS]
-                for j in range(TAPS):
-                    k = part * 5 + j
-                    sums[k] += (shifted[j][:ROWS] * inner).reshape(8, 8, 128).sum(0)
-                sums[part * 5 + 4] += inner.reshape(8, 8, 128).sum(0)
-            left[b, :, lanes] = jnp.where(x == 0, halves[0], halves[1]).astype(BF16)
+                gx_out[g, :, pl.ds(block * WIDTH + part * 128, 128)] = grad.astype(BF16)
+                mine = cell[:ROWS]
+                sums = [(shifted[j][:ROWS] * mine).sum(0, keepdims=True) for j in range(TAPS)]
+                sums.append(mine.sum(0, keepdims=True))
+                sums.append(jnp.zeros((3, 128), F32))
+                sums_out[feature, :, inner] = jnp.concatenate(sums, axis=0)
+
+        @pl.when(i < 16)
+        def _():
+            remote(
+                gx_out.at[g],
+                left.at[spot, :, pl.ds(0, 2 * WIDTH)],
+                gx_send,
+                gx_recv,
+                (dp, 2 * g + x),
+            ).start()
+
+        return 0
+
+    lax.fori_loop(1, 17, convolve, 0)
+    own_gx = local(gx_out.at[spot], left.at[spot, :, pl.ds(0, 2 * WIDTH)], load_sem.at[0])
+    own_gx.start()
+
+    gate_pair = remote(
+        gate_hbm.at[:, 1 - x],
+        left.at[:, :, pl.ds(3 * WIDTH, WIDTH)],
+        pair_send.at[0],
+        pair_recv.at[0],
+        partner,
+    )
+    gate_pair.start()
+
+    loads[4].wait()
+    loads[5].wait()
+
+    def gate_step(n, _):
+        for slot in range(2):
+
+            @pl.when(n > 0)
+            def _():
+                stage_wait(slot)
+
+            up_gradient(2 * n + slot, slot, gate_t, guz_hbm)
+        return 0
+
+    lax.fori_loop(0, 2, gate_step, 0)
+
+    def forward(q):
+        for copy in weight_copies(q):
+            copy.wait_recv()
+        for copy in forward_copies(q):
+            copy.start()
+
+    forward(0)
+
+    def hand_sums(step, _):
+        peer = group_peer(step)
         remote(
-            gx_buf.at[1 - x, b],
-            left.at[b, :, pl.ds(WIDTH, WIDTH)],
-            pair_send.at[1],
-            pair_recv.at[1],
-            partner,
+            sums_out.at[peer], sums_in.at[me], sums_send, sums_recv, (dp, peer)
         ).start()
-        return tuple(sums)
-
-    zero = jnp.zeros((8, 128), F32)
-    sums = lax.fori_loop(0, 16, convolve, (zero,) * 10)
-    for part in range(2):
-        rows = [sums[part * 5 + j].sum(0, keepdims=True) for j in range(5)]
-        rows.append(jnp.zeros((3, 128), F32))
-        small_ref[:, pl.ds(part * 128, 128)] = jnp.concatenate(rows, axis=0)
-
-    def turn_gx(b, _):
-        pair = jnp.concatenate([gx_buf[0, b], gx_buf[1, b]], axis=0).astype(F32)
-        gx_t[:, pl.ds(pl.multiple_of(b * 128, 128), 128)] = pair.T.astype(BF16)
         return 0
-
-    lax.fori_loop(0, 16, turn_gx, 0)
 
     def place(s, first):
         along_z = (1 - s) if first else s
@@ -404,22 +445,37 @@
                     value.astype(BF16)
                 )
 
+    def turn_gx(b, _):
+        pair = jnp.concatenate([left[b, :, pl.ds(0, WIDTH)], gx_far[b]], axis=0).astype(F32)
+        gx_t[:, pl.ds(pl.multiple_of(b * 128, 128), 128)] = pair.T.astype(BF16)
+        return 0
+
     def gx_step(n):
         for slot in range(2):
             stage_wait(slot)
             up_gradient(2 * n + slot, slot, gx_t, gux_hbm)
 
-    for i in (2, 3, 4):
-        loads[i].wait()
+    loads[6].wait()
+    loads[7].wait()
+    own_gx.wait()
+    far_spots = pl.ds(0, 15)
+    local(gx_out.at[far_spots], gx_out.at[far_spots], gx_recv).wait()
+    gx_pair = remote(
+        left.at[:, :, pl.ds(WIDTH, WIDTH)], gx_far, pair_send.at[1], pair_recv.at[1], partner
+    )
+    gx_pair.start()
     gate_pair.wait_recv()
-    own_part = left.at[:, :, pl.ds(WIDTH, WIDTH)]
-    local(own_part, own_part, pair_recv.at[1]).wait()
 
     first_terms(0)
     first_terms(1)
+    lax.fori_loop(1, GROUP, hand_sums, 0)
+    sums_in[me] = sums_out[me]
     passed_terms(0)
     first_terms(2)
     passed_terms(1)
+    lax.fori_loop(2, 4, gate_step, 0)
+    gx_pair.wait_recv()
+    lax.fori_loop(0, 16, turn_gx, 0)
     gx_step(0)
     own_terms(0)
     first_terms(3)
@@ -440,10 +496,16 @@
     finish(2)
     finish(3)
 
-    for k in range(2):
-        local(pre_buf.at[others], pre_buf.at[others], a2a_send.at[k]).wait()
+    local(sums_in.at[others], sums_in.at[others], sums_recv).wait()
+    small_ref[...] = sums_in[...].sum(0)
+
+    tail.wait_send()
+    head.wait_send()
+    local(params.at[others], params.at[others], param_send).wait()
+    local(sums_out.at[others], sums_out.at[others], sums_send).wait()
+    local(gx_out.at[far_spots], gx_out.at[far_spots], gx_send).wait()
     gate_pair.wait_send()
-    local(gx_buf.at[0], gx_buf.at[0], pair_send.at[1]).wait()
+    gx_pair.wait_send()
     for q in range(CHUNKS):
         for copy in weight_copies(q) + forward_copies(q):
             copy.wait_send()
@@ -468,24 +530,38 @@
         in_specs=[anywhere] * 4 + [vmem] * 2 + [anywhere] * 2,
         out_specs=(vmem, anywhere, anywhere, vmem),
         scratch_shapes=[
-            pltpu.VMEM((TOKENS + 16, WIDTH), BF16),
-            pltpu.VMEM((TOKENS + 32, WIDTH), BF16),
-            pltpu.VMEM((16, 2, ROWS, WIDTH), BF16),
+            pltpu.VMEM((ROWS, INNER), BF16),
+            pltpu.VMEM((ROWS, INNER), BF16),
+            pltpu.VMEM((2, 8, HALF // 2), F32),
+            pltpu.VMEM((2, 8, HALF // 2), F32),
+            pltpu.VMEM((16, HALF), BF16),
+            pltpu.VMEM((16, HALF), BF16),
+            pltpu.VMEM((GROUP, 8, WIDTH), F32),
+            pltpu.VMEM((GROUP, 8, WIDTH), F32),
+            pltpu.VMEM((GROUP, 8, WIDTH), F32),
+            pltpu.VMEM((16, ROWS, WIDTH), BF16),
             pltpu.VMEM((WIDTH, TOKENS), BF16),
-            pltpu.VMEM((2, 16, ROWS, WIDTH), BF16),
+            pltpu.VMEM((16, ROWS, 2 * WIDTH), BF16),
+            pltpu.VMEM((16, ROWS, WIDTH), BF16),
             pltpu.VMEM((WIDTH, TOKENS), BF16),
             pltpu.VMEM((16, ROWS, 4 * WIDTH), BF16),
             pltpu.VMEM((DIM, 4 * WIDTH), BF16),
-            pltpu.VMEM((TOKENS, DIM), BF16),
+            pltpu.VMEM((16, 2, ROWS, DIM), BF16),
             pltpu.VMEM((2, 512, WIDTH), F32),
             pltpu.VMEM((CHUNKS, 2, 6, 256, TILE), BF16),
             pltpu.VMEM((CHUNKS, 2, 6, 256, TILE), BF16),
             pltpu.VMEM((CHUNKS, 2, 6, ROWS, TILE), BF16),
             pltpu.VMEM((CHUNKS, 2, 6, ROWS, TILE), BF16),
             pltpu.VMEM((CHUNKS, 2, 2, 4, ROWS, TILE), F32),
-            dma((7,)),
+            dma((8,)),
+            dma,
+            dma,
             dma((2,)),
             dma((2,)),
+            dma,
+            dma,
+            dma,
+            dma,
             dma((CHUNKS, 2)),
             dma((CHUNKS, 2)),
             dma((CHUNKS, 2)),
@@ -506,7 +582,7 @@
         grad_act,
         x_pre,
         grad_gate.reshape(16, 2, ROWS, WIDTH),
-        normed_input,
+        normed_input.reshape(16, 2, ROWS, DIM),
         conv_weight,
         conv_bias.reshape(1, WIDTH),
         up_x,

time: 119 us -> 104 us (0.87)
  Pallas kernels: 106 us -> 91 us
    pallas_call x1, Pallas kernels: 106 us -> 91 us  [per_device(): pl.pallas_call(kernel, out_shape=(jax.ShapeDtypeStruct((ROWS, DIM), BF16)...]
where the time goes in v2:
time: 104 us; the launch traced here: 103 us
  Pallas kernels  91 us (88%)
  local copies, waits for them, and re-layouts  11.1 us (11%)
    pallas_call x1, Pallas kernels, per_device(): pl.pallas_call(kernel, out_shape=(jax.ShapeDtypeStruct((ROWS, DIM), BF16)...  91 us
    unnamed x5, local copies, waits for them, and re-layouts  8.52 us
    slice x2, local copies, waits for them, and re-layouts, per_device(): return (out, gux, guz, small[:TAPS], small[TAPS])  2.55 us

profile of v2, /device:TPU:0, one launch (start us, length us, event | category | flops | bytes accessed | tf_op | source)
XLA Modules:
  0.0 102.8 jit_solution(23924129189987487)
XLA Ops:
  0.6 91.0 %conv_up_backward.1 = (bf16[64,4096]{1,0:T(8,128)(2,1)}, f32[4096,256]{1,0:T(8,128)}, f32[4096,256]{1,0:T(8,128)}, f32[8,256]{1,0:T(8,128)}) custom-call(bf16[64,8192]{1,0:T(8,128)(2,1)} %act_hbm.1, bf16[64,8192]{1,0:T(8,128)(2,1)} %pre_hbm.1, bf16[16,2,64,256]{3,2,1,0:T(8,128)(2,1)} %bitcast.5, bf16[16,2,64,4096]{3,2,1,0:T(8,128)(2,1)} %bitcast.4, ...), custom_call_target="tpu_custom_call" | custom-call | tf_op jit(solution)/shard_map/conv_up_backward/pallas_call | solution.py:522
  91.7 1.3 %slice.7 = f32[1,256]{1,0:T(1,128)} slice(f32[8,256]{1,0:T(8,128)} %get-tuple-element.12), slice={[4:5], [0:256]} | slice | bytes 2048 | tf_op jit(solution)/shard_map/slice | solution.py:591
  92.9 1.3 %slice.6 = f32[4,256]{1,0:T(4,128)} slice(f32[8,256]{1,0:T(8,128)} %get-tuple-element.12), slice={[0:4], [0:256]} | slice | bytes 8192 | tf_op jit(solution)/shard_map/slice | solution.py:591
  94.2 1.9 %copy.16 = bf16[64,4096]{1,0:T(8,128)(2,1)} copy(bf16[64,4096]{1,0:T(8,128)(2,1)} %get-tuple-element.18) | data formatting | bytes 1048576
  96.1 0.0 copy-start
  96.1 4.6 %copy.17 = f32[4096,256]{1,0:T(8,128)} copy(f32[4096,256]{1,0:T(8,128)} %get-tuple-element.19) | data formatting | bytes 8388608
  100.7 0.0 copy-done
  100.7 2.0 %copy.18 = f32[4096,256]{1,0:T(8,128)} copy(f32[4096,256]{1,0:T(8,128)S(1)} %copy-done) | data formatting | bytes 8388608
Async XLA Ops:
  96.1 4.6 %copy-start = (f32[4096,256]{1,0:T(8,128)S(1)}, f32[4096,256]{1,0:T(8,128)}, u32[]{:S(2)}) copy-start(f32[4096,256]{1,0:T(8,128)} %get-tuple-element.20) | copy-start | bytes 12582916

commit v3 on v2

--- a/solution.py
+++ b/solution.py
@@ -18,6 +18,7 @@
 TOKENS = GROUP * ROWS
 CHUNKS = 4
 CHUNK = DIM // CHUNKS
+PIECES = 4
 TILE = CHUNK // 4
 
 
@@ -43,6 +44,8 @@
     params,
     sums_out,
     sums_in,
+    pair_out,
+    pair_in,
     gate_far,
     gate_t,
     gx_out,
@@ -87,8 +90,11 @@
     outside = ((dp + 2) % 4, me + 1 - 2 * x)
     sibling = (dp + 1 - 2 * core, me)
 
-    def group_peer(step):
-        return (me + step) % GROUP
+    def same_x(step):
+        return (dp, (spot + step) % 16 * 2 + x)
+
+    def other_x(step):
+        return (dp, (spot + step) % 16 * 2 + 1 - x)
 
     def local(src, dst, sem):
         return pltpu.make_async_copy(src, dst, sem)
@@ -118,54 +124,68 @@
 
     barrier = pltpu.get_barrier_semaphore()
 
-    def greet(step, _):
-        pl.semaphore_signal(
-            barrier, inc=1, device_id=(dp, group_peer(step)), device_id_type=MESH
-        )
+    def greet(device):
+        pl.semaphore_signal(barrier, inc=1, device_id=device, device_id_type=MESH)
+
+    def greet_step(step, _):
+        greet(same_x(step))
+        greet(other_x(step))
         return 0
 
-    lax.fori_loop(1, GROUP, greet, 0)
-    pl.semaphore_signal(barrier, inc=1, device_id=outside, device_id_type=MESH)
-    pl.semaphore_signal(barrier, inc=1, device_id=sibling, device_id_type=MESH)
+    greet(partner)
+    greet(sibling)
+    greet(outside)
+    lax.fori_loop(1, 16, greet_step, 0)
 
     loads[0].wait()
     loads[1].wait()
     top = lax.broadcasted_iota(jnp.int32, (8, 1024), 0) < 4
+    for part in range(2):
+        last = []
+        for k in (part, part + 2):
+            low = pre_buf[pl.ds(48, 16), pl.ds(k * 1024, 1024)].astype(F32)[8:]
+            high = pre_buf[pl.ds(48, 16), pl.ds(HALF + k * 1024, 1024)].astype(F32)[8:]
+            last.append(jnp.where(top, pltpu.roll(low, 4, 0), high))
+        tail_out[:, pl.ds(part * 1024, 1024)] = jnp.concatenate(last, axis=0).astype(BF16)
     for part in range(4):
-        low = pl.ds(part * 1024, 1024)
-        high = pl.ds(HALF + part * 1024, 1024)
-        last = pre_buf[pl.ds(48, 16), low].astype(F32)[8:]
-        last_high = pre_buf[pl.ds(48, 16), high].astype(F32)[8:]
-        last = jnp.where(top, pltpu.roll(last, 4, 0), last_high)
-        tail_out[part // 2, :, pl.ds((part % 2) * 1024, 1024)] = last
         first = []
         for buf in (pre_buf, act_buf):
-            rows = buf[pl.ds(0, 16), low].astype(F32)[:8]
-            rows_high = buf[pl.ds(0, 16), high].astype(F32)[:8]
-            first.append(jnp.where(top, rows, pltpu.roll(rows_high, 4, 0)))
-        head_out[:, low] = jnp.concatenate(first, axis=0).astype(BF16)
+            low = buf[pl.ds(0, 16), pl.ds(part * 1024, 1024)].astype(F32)[:8]
+            high = buf[pl.ds(0, 16), pl.ds(HALF + part * 1024, 1024)].astype(F32)[:8]
+            first.append(jnp.where(top, low, pltpu.roll(high, 4, 0)))
+        head_out[:, pl.ds(part * 1024, 1024)] = jnp.concatenate(first, axis=0).astype(BF16)
     params[me, pl.ds(0, TAPS), :] = taps_ref[...]
     params[me, pl.ds(TAPS, 1), :] = bias_ref[...]
     params[me, pl.ds(TAPS + 1, 3), :] = jnp.zeros((3, WIDTH), F32)
 
     pl.semaphore_wait(barrier, GROUP + 1)
 
-    tail = remote(
-        tail_out, tail_in, halo_send.at[0], halo_recv.at[0], (dp, group_peer(1))
-    )
-    head = remote(
-        head_out, head_in, halo_send.at[1], halo_recv.at[1], (dp, group_peer(GROUP - 1))
-    )
+    after_me = (dp, (me + 1) % GROUP)
+    before_me = (dp, (me + GROUP - 1) % GROUP)
+    tail = remote(tail_out, tail_in, halo_send.at[0], halo_recv.at[0], after_me)
+    head = remote(head_out, head_in, halo_send.at[1], halo_recv.at[1], before_me)
     tail.start()
     head.start()
 
+    def share_with(device):
+        remote(params.at[me], params.at[me], param_send, param_recv, device).start()
+
     def share(step, _):
-        remote(
-            params.at[me], params.at[me], param_send, param_recv, (dp, group_peer(step))
-        ).start()
+        share_with(same_x(step))
+        share_with(other_x(step))
         return 0
 
-    lax.fori_loop(1, GROUP, share, 0)
+    lax.fori_loop(1, 16, share, 0)
+    share_with(partner)
+
+    gate_pair = remote(
+        gate_hbm.at[:, 1 - x],
+        left.at[:, :, pl.ds(3 * WIDTH, WIDTH)],
+        pair_send.at[0],
+        pair_recv.at[0],
+        partner,
+    )
+    gate_pair.start()
 
     def weight_rows(q, half):
         return pl.ds(pl.multiple_of(q * CHUNK + half * (CHUNK // 2), CHUNK // 2), CHUNK // 2)
@@ -178,7 +198,7 @@
                 right.at[rows, pl.ds(slot * WIDTH, WIDTH)],
                 w_send.at[q, k],
                 w_recv.at[q, k],
-                outside,
+                outside if q < CHUNKS - 1 else partner,
             )
             for k, (src, slot) in enumerate(((upx_hbm, 1), (upz_hbm, 3)))
         ]
@@ -226,8 +246,14 @@
     others = pl.ds(0, GROUP - 1)
     local(params.at[others], params.at[others], param_recv).wait()
 
-    def convolve(i, _):
-        g = (spot + i) % 16
+    def skip_two(v):
+        return v + v // 2
+
+    def convolve(n, _):
+        rest = 15 - n
+        dz = jnp.where(n < 4, 2, jnp.where(n < 7, skip_two(n - 4), skip_two(rest // 3)))
+        dy = jnp.where(n < 4, n, jnp.where(n < 7, 2, skip_two(rest % 3)))
+        g = (z + dz) % 4 * 4 + (y + dy) % 4
         lower = g < 8
         for block in range(2):
             feature = 2 * g + (x + block) % 2
@@ -239,10 +265,9 @@
                 weights = [params[feature, pl.ds(j, 1), inner] for j in range(TAPS)]
                 bias = params[feature, pl.ds(TAPS, 1), inner]
                 before = tail_in[
-                    (feature % 16) // 8,
-                    :,
-                    pl.ds(pl.multiple_of((feature % 8) * WIDTH + part * 128, 128), 128),
-                ]
+                    :, pl.ds(pl.multiple_of((feature % 8) * WIDTH + part * 128, 128), 128)
+                ].astype(F32)
+                before = jnp.where((feature % 16) < 8, before[:8], before[8:])
                 before = jnp.where(lower, pltpu.roll(before, 4, 0), before)
                 before = jnp.where(me == 0, 0.0, before)
                 after = head_in[:, pl.ds(packed, 128)].astype(F32)
@@ -271,32 +296,23 @@
                 sums = [(shifted[j][:ROWS] * mine).sum(0, keepdims=True) for j in range(TAPS)]
                 sums.append(mine.sum(0, keepdims=True))
                 sums.append(jnp.zeros((3, 128), F32))
-                sums_out[feature, :, inner] = jnp.concatenate(sums, axis=0)
-
-        @pl.when(i < 16)
+                sums_out[g, block, :, inner] = jnp.concatenate(sums, axis=0)
+
+        @pl.when(n < 15)
         def _():
             remote(
                 gx_out.at[g],
                 left.at[spot, :, pl.ds(0, 2 * WIDTH)],
                 gx_send,
-                gx_recv,
+                gx_recv.at[spot],
                 (dp, 2 * g + x),
             ).start()
 
         return 0
 
-    lax.fori_loop(1, 17, convolve, 0)
+    lax.fori_loop(0, 16, convolve, 0)
     own_gx = local(gx_out.at[spot], left.at[spot, :, pl.ds(0, 2 * WIDTH)], load_sem.at[0])
     own_gx.start()
-
-    gate_pair = remote(
-        gate_hbm.at[:, 1 - x],
-        left.at[:, :, pl.ds(3 * WIDTH, WIDTH)],
-        pair_send.at[0],
-        pair_recv.at[0],
-        partner,
-    )
-    gate_pair.start()
 
     loads[4].wait()
     loads[5].wait()
@@ -322,11 +338,13 @@
     forward(0)
 
     def hand_sums(step, _):
-        peer = group_peer(step)
+        device = same_x(step)
         remote(
-            sums_out.at[peer], sums_in.at[me], sums_send, sums_recv, (dp, peer)
+            sums_out.at[(spot + step) % 16], sums_in.at[spot], sums_send, sums_recv, device
         ).start()
         return 0
+
+    sums_pair = remote(pair_out, pair_in, pair_send.at[2], pair_recv.at[2], partner)
 
     def place(s, first):
         along_z = (1 - s) if first else s
@@ -370,9 +388,12 @@
             neighbour(s, False, step),
         )
 
+    def gx_arrived(dz, dy):
+        source = (z + dz) % 4 * 4 + (y + dy) % 4
+        block = left.at[source, :, pl.ds(0, 2 * WIDTH)]
+        local(block, block, gx_recv.at[source]).wait()
+
     def first_terms(q):
-        if q > 0:
-            forward(q)
         for copy in forward_copies(q):
             copy.wait_recv()
 
@@ -385,7 +406,22 @@
             hop1(q, s, k).start()
             return 0
 
-        lax.fori_loop(0, 8, body, 0)
+        if q > 0:
+            lax.fori_loop(0, 8, body, 0)
+            return
+        for dy in range(4):
+            gx_arrived(2, dy)
+        lax.fori_loop(0, 2, lambda i, _: body(2 * i, _), 0)
+        for dz in (0, 1, 3):
+            gx_arrived(dz, 2)
+        lax.fori_loop(0, 2, lambda i, _: body(2 * i + 1, _), 0)
+        own_gx.wait()
+        for dz in (0, 1, 3):
+            for dy in (0, 1, 3):
+                if dz or dy:
+                    gx_arrived(dz, dy)
+        gx_pair.start()
+        lax.fori_loop(4, 8, body, 0)
 
     def passed_terms(q):
         def body(i, _):
@@ -457,23 +493,23 @@
 
     loads[6].wait()
     loads[7].wait()
-    own_gx.wait()
     far_spots = pl.ds(0, 15)
-    local(gx_out.at[far_spots], gx_out.at[far_spots], gx_recv).wait()
     gx_pair = remote(
         left.at[:, :, pl.ds(WIDTH, WIDTH)], gx_far, pair_send.at[1], pair_recv.at[1], partner
     )
-    gx_pair.start()
     gate_pair.wait_recv()
 
     first_terms(0)
+    forward(1)
     first_terms(1)
-    lax.fori_loop(1, GROUP, hand_sums, 0)
-    sums_in[me] = sums_out[me]
+    lax.fori_loop(1, 16, hand_sums, 0)
+    sums_in[spot] = sums_out[spot]
     passed_terms(0)
+    forward(2)
+    forward(3)
+    lax.fori_loop(2, 4, gate_step, 0)
     first_terms(2)
     passed_terms(1)
-    lax.fori_loop(2, 4, gate_step, 0)
     gx_pair.wait_recv()
     lax.fori_loop(0, 16, turn_gx, 0)
     gx_step(0)
@@ -485,6 +521,10 @@
     passed_rows(0)
     passed_terms(3)
     gx_step(2)
+    local(sums_in.at[far_spots], sums_in.at[far_spots], sums_recv).wait()
+    small_ref[...] = sums_in[:, 0].sum(0)
+    pair_out[...] = sums_in[:, 1].sum(0)
+    sums_pair.start()
     own_terms(2)
     passed_rows(1)
     finish(0)
@@ -496,13 +536,14 @@
     finish(2)
     finish(3)
 
-    local(sums_in.at[others], sums_in.at[others], sums_recv).wait()
-    small_ref[...] = sums_in[...].sum(0)
+    sums_pair.wait_recv()
+    small_ref[...] = small_ref[...] + pair_in[...]
 
     tail.wait_send()
     head.wait_send()
     local(params.at[others], params.at[others], param_send).wait()
-    local(sums_out.at[others], sums_out.at[others], sums_send).wait()
+    local(sums_out.at[far_spots], sums_out.at[far_spots], sums_send).wait()
+    sums_pair.wait_send()
     local(gx_out.at[far_spots], gx_out.at[far_spots], gx_send).wait()
     gate_pair.wait_send()
     gx_pair.wait_send()
@@ -513,6 +554,43 @@
     local(send2, send2, s2_send).wait()
     for slot in range(2):
         stage_wait(slot)
+
+
+def deliver(
+    rows_ref, gux_ref, guz_ref, small_ref, rows_out, gux_out, guz_out, taps_out, bias_out, hold, sem
+):
+    pieces = PIECES
+    depth = DIM // pieces
+    pairs = []
+    for k in range(pieces):
+        part = pl.ds(k * depth, depth)
+        pairs.append((gux_ref.at[part], hold.at[0, part], gux_out.at[part]))
+        pairs.append((guz_ref.at[part], hold.at[1, part], guz_out.at[part]))
+    reads = [
+        pltpu.make_async_copy(src, mid, sem.at[0, k]) for k, (src, mid, _) in enumerate(pairs)
+    ]
+    writes = [
+        pltpu.make_async_copy(mid, dst, sem.at[1, k]) for k, (_, mid, dst) in enumerate(pairs)
+    ]
+    for copy in reads:
+        copy.start()
+    small = [
+        pltpu.make_async_copy(src, dst, sem.at[k, 2 * pieces])
+        for k, (src, dst) in enumerate(
+            (
+                (rows_ref, rows_out),
+                (small_ref.at[pl.ds(0, TAPS)], taps_out),
+                (small_ref.at[pl.ds(TAPS, 1)], bias_out),
+            )
+        )
+    ]
+    for copy in small:
+        copy.start()
+    for read, write in zip(reads, writes):
+        read.wait()
+        write.start()
+    for copy in writes + small:
+        copy.wait()
 
 
 def per_device(grad_act, x_pre, grad_gate, normed_input, conv_weight, conv_bias, up_x, up_z):
@@ -532,13 +610,15 @@
         scratch_shapes=[
             pltpu.VMEM((ROWS, INNER), BF16),
             pltpu.VMEM((ROWS, INNER), BF16),
-            pltpu.VMEM((2, 8, HALF // 2), F32),
-            pltpu.VMEM((2, 8, HALF // 2), F32),
+            pltpu.VMEM((16, HALF // 2), BF16),
+            pltpu.VMEM((16, HALF // 2), BF16),
             pltpu.VMEM((16, HALF), BF16),
             pltpu.VMEM((16, HALF), BF16),
             pltpu.VMEM((GROUP, 8, WIDTH), F32),
-            pltpu.VMEM((GROUP, 8, WIDTH), F32),
-            pltpu.VMEM((GROUP, 8, WIDTH), F32),
+            pltpu.VMEM((16, 2, 8, WIDTH), F32),
+            pltpu.VMEM((16, 2, 8, WIDTH), F32),
+            pltpu.VMEM((8, WIDTH), F32),
+            pltpu.VMEM((8, WIDTH), F32),
             pltpu.VMEM((16, ROWS, WIDTH), BF16),
             pltpu.VMEM((WIDTH, TOKENS), BF16),
             pltpu.VMEM((16, ROWS, 2 * WIDTH), BF16),
@@ -559,15 +639,15 @@
             dma((2,)),
             dma((2,)),
             dma,
-            dma,
+            dma((16,)),
             dma,
             dma,
             dma((CHUNKS, 2)),
             dma((CHUNKS, 2)),
             dma((CHUNKS, 2)),
             dma((CHUNKS, 2)),
-            dma((2,)),
-            dma((2,)),
+            dma((3,)),
+            dma((3,)),
             dma((2,)),
             dma,
             dma((CHUNKS, 2, 6)),
@@ -588,7 +668,22 @@
         up_x,
         up_z,
     )
-    return out, gux, guz, small[:TAPS], small[TAPS]
+    out, gux, guz, taps, bias = pl.pallas_call(
+        deliver,
+        out_shape=(
+            jax.ShapeDtypeStruct((ROWS, DIM), BF16),
+            jax.ShapeDtypeStruct((DIM, WIDTH), F32),
+            jax.ShapeDtypeStruct((DIM, WIDTH), F32),
+            jax.ShapeDtypeStruct((TAPS, WIDTH), F32),
+            jax.ShapeDtypeStruct((1, WIDTH), F32),
+        ),
+        in_specs=[vmem, anywhere, anywhere, vmem],
+        out_specs=(anywhere,) * 5,
+        scratch_shapes=[pltpu.VMEM((2, DIM, WIDTH), F32), dma((3, 2 * PIECES + 1))],
+        compiler_params=pltpu.CompilerParams(vmem_limit_bytes=62 * 1024 * 1024),
+        name="deliver",
+    )(out, gux, guz, small)
+    return out, gux, guz, taps, bias.reshape(WIDTH)
 
 
 def solution(mesh):

time: 104 us -> 94.3 us (0.907); the launches traced: 103 us -> 94.2 us
  local copies, waits for them, and re-layouts: 11.1 us -> 0 us
  Pallas kernels: 91 us -> 93.5 us
    unnamed x5 -> x0, local copies, waits for them, and re-layouts: 8.52 us -> none
    pallas_call x0 -> x1, Pallas kernels: none -> 7.76 us  [per_device(): pl.pallas_call(deliver, out_shape=(jax.ShapeDtypeStruct((ROWS, DIM), BF16...]
    pallas_call x1, Pallas kernels: 91 us -> 85.8 us  [per_device(): pl.pallas_call(kernel, out_shape=(jax.ShapeDtypeStruct((ROWS, DIM), BF16)...]
    slice x2 -> x0, local copies, waits for them, and re-layouts: 2.55 us -> none  [per_device(): return (out, gux, guz, small[:TAPS], small[TAPS])]
where the time goes in v3:
time: 94.3 us; the launch traced here: 94.2 us
  Pallas kernels  93.5 us (99%)
    pallas_call x1, Pallas kernels, per_device(): pl.pallas_call(kernel, out_shape=(jax.ShapeDtypeStruct((ROWS, DIM), BF16)...  85.8 us
    pallas_call x1, Pallas kernels, per_device(): pl.pallas_call(deliver, out_shape=(jax.ShapeDtypeStruct((ROWS, DIM), BF16...  7.76 us

profile of v3, /device:TPU:0, one launch (start us, length us, event | category | flops | bytes accessed | tf_op | source)
XLA Modules:
  0.0 94.2 jit_solution(2551816948939412451)
XLA Ops:
  0.6 85.8 %conv_up_backward.1 = (bf16[64,4096]{1,0:T(8,128)(2,1)}, f32[4096,256]{1,0:T(8,128)}, f32[4096,256]{1,0:T(8,128)}, f32[8,256]{1,0:T(8,128)}) custom-call(bf16[64,8192]{1,0:T(8,128)(2,1)} %act_hbm.1, bf16[64,8192]{1,0:T(8,128)(2,1)} %pre_hbm.1, bf16[16,2,64,256]{3,2,1,0:T(8,128)(2,1)} %bitcast.5, bf16[16,2,64,4096]{3,2,1,0:T(8,128)(2,1)} %bitcast.4, ...), custom_call_target="tpu_custom_call" | custom-call | tf_op jit(solution)/shard_map/conv_up_backward/pallas_call | solution.py:600
  86.4 7.8 %deliver.1 = (bf16[64,4096]{1,0:T(8,128)(2,1)}, f32[4096,256]{1,0:T(8,128)}, f32[4096,256]{1,0:T(8,128)}, f32[4,256]{1,0:T(4,128)}, f32[1,256]{1,0:T(1,128)}) custom-call(bf16[64,4096]{1,0:T(8,128)(2,1)} %get-tuple-element.14.rows_ref, f32[4096,256]{1,0:T(8,128)} %get-tuple-element.15.gux_ref, f32[4096,256]{1,0:T(8,128)} %get-tuple-element.16.guz_ref, ...), custom_call_target="tpu_custom_call" | custom-call | tf_op jit(solution)/shard_map/deliver/pallas_call | solution.py:671

commit v4 on v3

--- a/solution.py
+++ b/solution.py
@@ -27,14 +27,17 @@
     pre_hbm,
     gate_hbm,
     normed_hbm,
-    taps_ref,
-    bias_ref,
+    taps_hbm,
+    bias_hbm,
     upx_hbm,
     upz_hbm,
-    out_ref,
+    out_hbm,
     gux_hbm,
     guz_hbm,
     small_ref,
+    taps_buf,
+    bias_buf,
+    out_buf,
     act_buf,
     pre_buf,
     tail_out,
@@ -61,6 +64,7 @@
     recv2,
     total,
     load_sem,
+    out_sem,
     param_send,
     param_recv,
     halo_send,
@@ -118,8 +122,10 @@
         local(normed_hbm.at[:, 1 - x], normed.at[:, 1], load_sem.at[5]),
         local(upx_hbm, right.at[:, pl.ds(0, WIDTH)], load_sem.at[6]),
         local(upz_hbm, right.at[:, pl.ds(2 * WIDTH, WIDTH)], load_sem.at[7]),
+        local(taps_hbm, taps_buf, load_sem.at[8]),
+        local(bias_hbm, bias_buf, load_sem.at[9]),
     ]
-    for copy in loads:
+    for copy in loads[8:] + loads[:8]:
         copy.start()
 
     barrier = pltpu.get_barrier_semaphore()
@@ -154,8 +160,10 @@
             high = buf[pl.ds(0, 16), pl.ds(HALF + part * 1024, 1024)].astype(F32)[:8]
             first.append(jnp.where(top, low, pltpu.roll(high, 4, 0)))
         head_out[:, pl.ds(part * 1024, 1024)] = jnp.concatenate(first, axis=0).astype(BF16)
-    params[me, pl.ds(0, TAPS), :] = taps_ref[...]
-    params[me, pl.ds(TAPS, 1), :] = bias_ref[...]
+    loads[8].wait()
+    loads[9].wait()
+    params[me, pl.ds(0, TAPS), :] = taps_buf[...]
+    params[me, pl.ds(TAPS, 1), :] = bias_buf[...]
     params[me, pl.ds(TAPS + 1, 3), :] = jnp.zeros((3, WIDTH), F32)
 
     pl.semaphore_wait(barrier, GROUP + 1)
@@ -469,6 +477,10 @@
 
         lax.fori_loop(0, 4, body, 0)
 
+    def rows_out(q):
+        columns = pl.ds(q * CHUNK, CHUNK)
+        return local(out_buf.at[:, columns], out_hbm.at[:, columns], out_sem.at[q])
+
     def finish(q):
         for s in range(2):
             for half in range(2):
@@ -477,9 +489,10 @@
                 hop2(q, s, 3 + 2 * half).wait_recv()
                 value += recv2[q, s, 4 - 2 * half].astype(F32)
                 value += recv2[q, s, 3 + 2 * half].astype(F32)
-                out_ref[:, pl.ds(q * CHUNK + s * (CHUNK // 2) + half * TILE, TILE)] = (
+                out_buf[:, pl.ds(q * CHUNK + s * (CHUNK // 2) + half * TILE, TILE)] = (
                     value.astype(BF16)
                 )
+        rows_out(q).start()
 
     def turn_gx(b, _):
         pair = jnp.concatenate([left[b, :, pl.ds(0, WIDTH)], gx_far[b]], axis=0).astype(F32)
@@ -550,6 +563,8 @@
     for q in range(CHUNKS):
         for copy in weight_copies(q) + forward_copies(q):
             copy.wait_send()
+    for q in range(CHUNKS):
+        rows_out(q).wait()
     local(send1, send1, s1_send).wait()
     local(send2, send2, s2_send).wait()
     for slot in range(2):
@@ -557,39 +572,48 @@
 
 
 def deliver(
-    rows_ref, gux_ref, guz_ref, small_ref, rows_out, gux_out, guz_out, taps_out, bias_out, hold, sem
+    rows_ref,
+    gux_ref,
+    guz_ref,
+    small_ref,
+    rows_out,
+    gux_out,
+    guz_out,
+    taps_out,
+    bias_out,
+    hold,
+    rows_hold,
+    small_hold,
+    sem,
 ):
-    pieces = PIECES
-    depth = DIM // pieces
-    pairs = []
-    for k in range(pieces):
+    depth = DIM // PIECES
+    steps = [
+        (small_ref, small_hold, None),
+        (rows_ref, rows_hold, rows_out),
+    ]
+    for k in range(PIECES):
         part = pl.ds(k * depth, depth)
-        pairs.append((gux_ref.at[part], hold.at[0, part], gux_out.at[part]))
-        pairs.append((guz_ref.at[part], hold.at[1, part], guz_out.at[part]))
+        steps.append((gux_ref.at[part], hold.at[0, part], gux_out.at[part]))
+        steps.append((guz_ref.at[part], hold.at[1, part], guz_out.at[part]))
     reads = [
-        pltpu.make_async_copy(src, mid, sem.at[0, k]) for k, (src, mid, _) in enumerate(pairs)
-    ]
-    writes = [
-        pltpu.make_async_copy(mid, dst, sem.at[1, k]) for k, (_, mid, dst) in enumerate(pairs)
+        pltpu.make_async_copy(src, mid, sem.at[0, k]) for k, (src, mid, _) in enumerate(steps)
     ]
     for copy in reads:
         copy.start()
-    small = [
-        pltpu.make_async_copy(src, dst, sem.at[k, 2 * pieces])
-        for k, (src, dst) in enumerate(
-            (
-                (rows_ref, rows_out),
-                (small_ref.at[pl.ds(0, TAPS)], taps_out),
-                (small_ref.at[pl.ds(TAPS, 1)], bias_out),
-            )
-        )
-    ]
-    for copy in small:
-        copy.start()
-    for read, write in zip(reads, writes):
-        read.wait()
-        write.start()
-    for copy in writes + small:
+    writes = []
+    for k, (_, mid, dst) in enumerate(steps):
+        reads[k].wait()
+        if k == 0:
+            out = [
+                pltpu.make_async_copy(mid.at[pl.ds(0, TAPS)], taps_out, sem.at[1, 0]),
+                pltpu.make_async_copy(mid.at[pl.ds(TAPS, 1)], bias_out, sem.at[1, len(steps)]),
+            ]
+        else:
+            out = [pltpu.make_async_copy(mid, dst, sem.at[1, k])]
+        for copy in out:
+            copy.start()
+        writes += out
+    for copy in writes:
         copy.wait()
 
 
@@ -605,9 +629,12 @@
             jax.ShapeDtypeStruct((DIM, WIDTH), F32),
             jax.ShapeDtypeStruct((8, WIDTH), F32),
         ),
-        in_specs=[anywhere] * 4 + [vmem] * 2 + [anywhere] * 2,
-        out_specs=(vmem, anywhere, anywhere, vmem),
+        in_specs=[anywhere] * 8,
+        out_specs=(anywhere, anywhere, anywhere, vmem),
         scratch_shapes=[
+            pltpu.VMEM((TAPS, WIDTH), F32),
+            pltpu.VMEM((1, WIDTH), F32),
+            pltpu.VMEM((ROWS, DIM), BF16),
             pltpu.VMEM((ROWS, INNER), BF16),
             pltpu.VMEM((ROWS, INNER), BF16),
             pltpu.VMEM((16, HALF // 2), BF16),
@@ -633,7 +660,8 @@
             pltpu.VMEM((CHUNKS, 2, 6, ROWS, TILE), BF16),
             pltpu.VMEM((CHUNKS, 2, 6, ROWS, TILE), BF16),
             pltpu.VMEM((CHUNKS, 2, 2, 4, ROWS, TILE), F32),
-            dma((8,)),
+            dma((10,)),
+            dma((CHUNKS,)),
             dma,
             dma,
             dma((2,)),
@@ -677,9 +705,14 @@
             jax.ShapeDtypeStruct((TAPS, WIDTH), F32),
             jax.ShapeDtypeStruct((1, WIDTH), F32),
         ),
-        in_specs=[vmem, anywhere, anywhere, vmem],
+        in_specs=[anywhere] * 4,
         out_specs=(anywhere,) * 5,
-        scratch_shapes=[pltpu.VMEM((2, DIM, WIDTH), F32), dma((3, 2 * PIECES + 1))],
+        scratch_shapes=[
+            pltpu.VMEM((2, DIM, WIDTH), F32),
+            pltpu.VMEM((ROWS, DIM), BF16),
+            pltpu.VMEM((8, WIDTH), F32),
+            dma((2, 2 * PIECES + 3)),
+        ],
         compiler_params=pltpu.CompilerParams(vmem_limit_bytes=62 * 1024 * 1024),
         name="deliver",
     )(out, gux, guz, small)

time: 94.3 us -> 93.2 us (0.988)
  Pallas kernels: 93.5 us -> 92.4 us
    pallas_call x1, Pallas kernels: 7.76 us -> 6.79 us  [per_device(): pl.pallas_call(deliver, out_shape=(jax.ShapeDtypeStruct((ROWS, DIM), BF16...]
where the time goes in v4:
time: 93.2 us; the launch traced here: 93.1 us
  Pallas kernels  92.4 us (99%)
    pallas_call x1, Pallas kernels, per_device(): pl.pallas_call(kernel, out_shape=(jax.ShapeDtypeStruct((ROWS, DIM), BF16)...  85.6 us
    pallas_call x1, Pallas kernels, per_device(): pl.pallas_call(deliver, out_shape=(jax.ShapeDtypeStruct((ROWS, DIM), BF16...  6.79 us

profile of v4, /device:TPU:0, one launch (start us, length us, event | category | flops | bytes accessed | tf_op | source)
XLA Modules:
  0.0 93.1 jit_solution(10304440171482683719)
XLA Ops:
  0.6 85.6 %conv_up_backward.1 = (bf16[64,4096]{1,0:T(8,128)(2,1)}, f32[4096,256]{1,0:T(8,128)}, f32[4096,256]{1,0:T(8,128)}, f32[8,256]{1,0:T(8,128)}) custom-call(bf16[64,8192]{1,0:T(8,128)(2,1)} %act_hbm.1, bf16[64,8192]{1,0:T(8,128)(2,1)} %pre_hbm.1, bf16[16,2,64,256]{3,2,1,0:T(8,128)(2,1)} %bitcast.5, bf16[16,2,64,4096]{3,2,1,0:T(8,128)(2,1)} %bitcast.4, ...), custom_call_target="tpu_custom_call" | custom-call | tf_op jit(solution)/shard_map/conv_up_backward/pallas_call | solution.py:624
  86.3 6.8 %deliver.1 = (bf16[64,4096]{1,0:T(8,128)(2,1)}, f32[4096,256]{1,0:T(8,128)}, f32[4096,256]{1,0:T(8,128)}, f32[4,256]{1,0:T(4,128)}, f32[1,256]{1,0:T(1,128)}) custom-call(bf16[64,4096]{1,0:T(8,128)(2,1)} %get-tuple-element.14.rows_ref, f32[4096,256]{1,0:T(8,128)} %get-tuple-element.15.gux_ref, f32[4096,256]{1,0:T(8,128)} %get-tuple-element.16.guz_ref, ...), custom_call_target="tpu_custom_call" | custom-call | tf_op jit(solution)/shard_map/deliver/pallas_call | solution.py:699
